TPU v7x, 128 devices: a whole 4x4x4 slice. The times are simulated.
128 devices in a mesh: blk: 16 (over x, y), aux: 8 (over z, core).
Axes of the slice: x: 4, y: 4, z: 4, core: 2. Of those that a mesh axis runs over, the one named last changes fastest.
Arguments:
- factors: float32 [80, 256, 32, 256], P('blk', 'aux'), may hold values from -6 to 6
- partners: int32 [64, 10], replicated, may hold values from -1 to 63, as said below
- block_owner: int32 [64], replicated, may hold values from 0 to 15, as said below
Outputs:
- pair_blocks: float32 [80, 10, 256, 256], P('blk', None, 'aux')
- diag_blocks: float32 [80, 256, 256], P('blk', 'aux')
Inputs may be any that keep to these rules, and one draw needn't show every extreme that they name: `partners`: row a lists in increasing order the blocks c != a with |a - c| <= 5 that are significant with a, then -1 in the remaining slots; c is listed in row a exactly when a is listed in row c; some row lists 10 blocks. `block_owner`: never falls along the blocks; every index of blk holds 3 to 5 consecutive blocks, and some index holds exactly 5.
All inputs are finite; a program needn't handle non-finite values.
Results may differ from a plain program's by a relative error of at most 0.0003.
Values sent between devices are 32-bit elements; how exact they have to be, the bound alone decides.
A program may use at most 192 MiB of HBM per device.

v0:
```python
import math

import jax
import jax.numpy as jnp
from jax import lax
from jax.sharding import PartitionSpec as P

RMAX = 5
REACH = 2


def from_behind_2(value, axis, steps):
    count = lax.axis_size(axis)
    initial, last = (max(0, -steps), min(count, count - steps))
    return lax.ppermute(value, axis, [(source, source + steps) for source in range(initial, last)])


def lookup(table, positions):
    matches = positions[..., None] == jnp.arange(table.shape[0], dtype=jnp.int32)
    return jnp.sum(jnp.where(matches, table, 0), axis=-1)


def outer_sum(left, right):
    return jnp.einsum(
        "spm,spn->smn",
        left,
        right,
        precision=lax.Precision.HIGHEST,
        preferred_element_type=jnp.float32,
    )


def fetch_ahead(factors):
    slot_count = factors.shape[0]
    fetched = [from_behind_2(factors, "blk", -distance) for distance in range(1, REACH + 1)]
    starts = [slot_count * distance for distance in range(REACH + 1)]
    return (fetched, starts)


def local(factors, partners, block_owner):
    slot_count, aux_dev, occ_count, block_size = factors.shape
    blk_count = lax.axis_size("blk")
    scale_factor = 1.0 / math.sqrt(aux_dev * lax.axis_size("aux") * occ_count)
    block_total = block_owner.shape[0]
    partner_slots = partners.shape[1]
    device_index = lax.axis_index("blk")
    devices = jnp.arange(blk_count, dtype=jnp.int32)
    owned = block_owner[None, :] == devices[:, None]
    counts = jnp.sum(owned.astype(jnp.int32), axis=1)
    firsts = jnp.sum((block_owner[None, :] < devices[:, None]).astype(jnp.int32), axis=1)
    block_first = jnp.sum(jnp.where(owned, firsts[:, None], 0), axis=0)
    my_first = lookup(firsts, device_index)
    my_count = lookup(counts, device_index)
    slot_ids = jnp.arange(slot_count, dtype=jnp.int32)
    mine = jnp.minimum(my_first + slot_ids, block_total - 1)
    live = slot_ids < my_count
    local_rows = factors.reshape(slot_count, aux_dev * occ_count, block_size)
    diag_block = outer_sum(local_rows, local_rows) * scale_factor
    diag_block = jnp.where(live[:, None, None], diag_block, 0.0)
    fetched, starts = fetch_ahead(factors)
    group_starts = jnp.array(starts, dtype=jnp.int32)
    window = jnp.concatenate([factors] + fetched, axis=0).reshape(
        -1, aux_dev * occ_count, block_size
    )
    pair_list = []
    for offset in range(RMAX):
        target = jnp.minimum(mine + 1 + offset, block_total - 1)
        ahead = jnp.clip(lookup(block_owner, target) - device_index, 0, REACH)
        place = lookup(group_starts, ahead) + target - lookup(block_first, target)
        place = jnp.clip(place, 0, window.shape[0] - 1)
        pair_list.append(outer_sum(local_rows, jnp.take(window, place, axis=0)) * scale_factor)
    upper_pairs = jnp.stack(pair_list, axis=1)
    listed = jnp.take(partners, mine, axis=0)
    own_ids = mine[:, None]
    above = listed > own_ids
    below = (listed >= 0) & (listed < own_ids)
    keep_mask = live[:, None] & (above | below)
    clipped = jnp.clip(listed, 0, block_total - 1)
    distance_back = device_index - lookup(block_owner, clipped)
    partner_slot = clipped - lookup(block_first, clipped)
    group_size = slot_count * RMAX
    above_index = slot_ids[:, None] * RMAX + clipped - own_ids - 1
    below_index = distance_back * group_size + partner_slot * RMAX + own_ids - clipped - 1
    from_behind = [from_behind_2(upper_pairs, "blk", distance) for distance in range(1, REACH + 1)]
    candidates = jnp.concatenate([upper_pairs] + from_behind, axis=0).reshape(
        -1, block_size, block_size
    )
    picked = jnp.clip(jnp.where(above, above_index, below_index), 0, candidates.shape[0] - 1)
    chosen = jnp.take(candidates, picked.reshape(-1), axis=0).reshape(
        slot_count, partner_slots, block_size, block_size
    )
    chosen = jnp.where(below[:, :, None, None], jnp.swapaxes(chosen, 2, 3), chosen)
    chosen = jnp.where(keep_mask[:, :, None, None], chosen, 0.0)
    pair_part, diag_part = (
        lax.psum_scatter(chosen, "aux", scatter_dimension=2, tiled=True),
        lax.psum_scatter(diag_block, "aux", scatter_dimension=1, tiled=True),
    )
    return (pair_part, diag_part)


def solution(mesh):
    in_specs = (P("blk", "aux", None, None), P(), P())
    out_specs = (P("blk", None, "aux", None), P("blk", "aux", None))
    return jax.shard_map(local, mesh=mesh, in_specs=in_specs, out_specs=out_specs, check_vma=False)
```

profile of v0, /device:TPU:1, one launch (start us, length us, event | category | flops | bytes accessed | tf_op | source)
XLA Modules:
  0.0 1061.0 jit_solution(16515738551233746813)
XLA Ops:
  7.2 1.3 collective-permute-start
  8.5 1.3 collective-permute-start.1
  9.8 0.8 convert_reduce_fusion.1
  10.6 0.6 fusion.66
  11.2 0.7 add_minimum_fusion
  11.9 0.7 add_minimum_fusion.1
  12.5 0.7 add_minimum_fusion.2
  13.2 0.7 add_minimum_fusion.3
  13.9 0.7 add_minimum_fusion.4
  14.5 0.7 select_reduce_fusion.2
  15.3 1.0 select_reduce_fusion.4
  16.4 0.7 compare_and_fusion.6
  17.1 0.7 compare_and_fusion.5
  17.8 0.7 compare_and_fusion.4
  18.5 0.7 compare_and_fusion.3
  19.1 0.7 compare_and_fusion.2
  19.8 216.5 %collective-permute-done = f32[5,32,32,256]{3,2,1,0:T(8,128)} collective-permute-done((f32[5,32,32,256]{3,2,1,0:T(8,128)}, f32[5,32,32,256]{3,2,1,0:T(8,128)}, u32[]{:S(2)}, u32[]{:S(2)}) %collective-permute-start) | collective-permute-done | bytes 5242912 | tf_op jit(solution)/shard_map/ppermute | solution.py:15
  236.3 11.4 %pad_maximum_fusion.1 = f32[15,32,32,256]{3,2,1,0:T(8,128)} fusion(f32[5,32,32,256]{3,2,1,0:T(8,128)} %collective-permute-done.1, f32[5,32,32,256]{3,2,1,0:T(8,128)} %collective-permute-done, f32[5,32,32,256]{3,2,1,0:T(8,128)} %param.6), kind=kLoop, calls=%fused_computation.8 | loop fusion | flops 7864320 | bytes 31457280 | tf_op jit(solution)/shard_map/concatenate | solution.py:62
  247.6 8.8 gather_fusion.2
  256.4 8.6 gather_fusion.3
  265.0 8.7 gather_fusion.4
  273.7 8.6 gather_fusion.5
  282.3 8.8 gather_fusion.6
  291.2 13.8 %fusion.27 = f32[5,5,256,256]{2,3,0,1:T(8,128)} fusion(f32[5,1024,256]{2,1,0:T(8,128)} %bitcast.47, f32[5,1024,256]{2,1,0:T(8,128)} %gather_fusion.2, pred[5]{0:T(512)(128)(4,1)S(1)} %get-tuple-element.36), kind=kOutput, calls=%fused_computation.35 | convolution fusion | flops 4028170240 | bytes 11796485 | tf_op jit(solution)/shard_map/spm,spn->smn/dot_general | solution.py:24
  305.0 12.6 %fusion.36 = f32[5,5,256,256]{2,3,0,1:T(8,128)} fusion(f32[5,5,256,256]{2,3,0,1:T(8,128)} %fusion.27, f32[5,1024,256]{2,1,0:T(8,128)S(1)} %bitcast.50, f32[5,1024,256]{2,1,0:T(8,128)} %gather_fusion.3, pred[5]{0:T(512)(128)(4,1)S(1)} %get-tuple-element.34), kind=kOutput, calls=%fused_computation.38 | convolution fusion | flops 4028170240 | bytes 11796485 | tf_op jit(solution)/shard_map/spm,spn->smn/dot_general | solution.py:24
  317.6 9.8 fusion.45
  327.4 9.7 fusion.54
  337.1 9.9 fusion.63
  347.0 7.1 collective-permute-start.2
  354.1 117.3 %collective-permute-start.3 = (f32[5,5,256,256]{2,3,0,1:T(8,128)}, f32[5,5,256,256]{2,3,0,1:T(8,128)}, u32[]{:S(2)}, u32[]{:S(2)}) collective-permute-start(f32[5,5,256,256]{2,3,0,1:T(8,128)} %fusion.63), channel_id=1, source_target_pairs={{0,16},{8,24},{16,32},{24,40},{32,48},{40,56},{48,64},{56,72},{64,... | collective-permute-start | bytes 19660808 | tf_op jit(solution)/shard_map/ppermute | solution.py:15
  471.4 0.7 iota_compare_fusion.13
  472.1 9.5 fusion.20
  481.7 0.3 reduce-scatter.3.cloned.1.call-start
  482.0 0.1 copy.18
  482.1 0.7 fusion.69
  482.8 0.6 gather_fusion
  483.3 0.7 add_minimum_fusion.5
  484.0 0.7 compare_and_fusion.7
  484.8 0.3 select_reduce_fusion
  485.7 4.9 collective-permute-done.2
  490.6 140.5 %collective-permute-done.3 = f32[5,5,256,256]{2,3,0,1:T(8,128)} collective-permute-done((f32[5,5,256,256]{2,3,0,1:T(8,128)}, f32[5,5,256,256]{2,3,0,1:T(8,128)}, u32[]{:S(2)}, u32[]{:S(2)}) %collective-permute-start.3) | collective-permute-done | bytes 6553632 | tf_op jit(solution)/shard_map/ppermute | solution.py:15
  631.1 15.3 %pad_maximum_fusion = f32[15,5,256,256]{2,3,0,1:T(8,128)} fusion(f32[5,5,256,256]{2,3,0,1:T(8,128)} %collective-permute-done.3, f32[5,5,256,256]{2,3,0,1:T(8,128)} %collective-permute-done.2, f32[5,5,256,256]{2,3,0,1:T(8,128)} %fusion.63), kind=kLoop, calls=%fused_computation.7 | loop fusion | flops 9830400 | bytes 39321600 | tf_op jit(solution)/shard_map/concatenate | solution.py:85
  646.4 21.5 %copy.24 = f32[15,5,256,256]{3,2,1,0:T(8,128)} copy(f32[15,5,256,256]{2,3,0,1:T(8,128)} %pad_maximum_fusion) | data formatting | bytes 39321600 | tf_op jit(solution)/shard_map/concatenate | solution.py:85
  668.0 14.3 %gather_fusion.1 = f32[50,256,256]{2,1,0:T(8,128)} fusion(f32[75,256,256]{2,1,0:T(8,128)} %bitcast.62, s32[1024]{0:T(1024)S(1)} %pad_clamp_fusion), kind=kCustom, calls=%fused_computation.6 | custom fusion | bytes 26214600 | tf_op jit(solution)/shard_map/jit(_take)/gather | solution.py:89
  682.3 12.0 %select_bitcast_fusion = f32[5,10,256,256]{2,3,1,0:T(8,128)} fusion(f32[5,10,256,256]{3,2,1,0:T(8,128)} %bitcast.55, pred[5,10]{1,0:T(8,128)(4,1)S(1)} %get-tuple-element.26), kind=kLoop, calls=%fused_computation.10 | loop fusion | flops 3276800 | bytes 26214450 | tf_op jit(solution)/shard_map/transpose | solution.py:92
  694.3 13.9 %copy.25 = f32[5,10,256,256]{3,2,1,0:T(8,128)} copy(f32[5,10,256,256]{2,3,1,0:T(8,128)} %select_bitcast_fusion) | data formatting | bytes 26214400 | tf_op jit(solution)/shard_map/transpose | solution.py:92
  708.2 14.0 %select_select_fusion = f32[5,10,256,256]{3,2,1,0:T(8,128)} fusion(f32[5,10,256,256]{3,2,1,0:T(8,128)} %copy.25, f32[5,10,256,256]{3,2,1,0:T(8,128)} %bitcast.56, pred[5,10]{1,0:T(8,128)(4,1)S(1)} %get-tuple-element.26, pred[5,10]{1,0:T(8,128)(4,1)S(1)} %get-tuple-element.23, pred[5,10]{1,0:T(8,128)(4,1)S(1)} %get-tuple-element.22), kind=kLoop, calls=%fused_computation.9 | loop fusion | flops 9830400 | bytes 39321752 | tf_op jit(solution)/shard_map/jit(_where)/select_n | solution.py:93
  722.2 331.5 %reduce-scatter.3.cloned.1.call-done = f32[5,10,32,256]{3,2,1,0:T(8,128)} async-done(((f32[5,10,256,256]{3,2,1,0:T(8,128)}), f32[5,10,32,256]{3,2,1,0:T(8,128)}) %reduce-scatter.3.cloned.1.call-update) | async-done | bytes 1638416 | tf_op jit(solution)/shard_map/reduce_scatter | solution.py:95
  (55 shorter events, 1.0 us)
Async XLA Ops:
  7.2 715.1 %reduce-scatter.5.cloned.1.call-start = ((), (), s32[]{:S(2)}) async-start(), calls=%async_computation.3 | async-start | bytes 1474560 | tf_op jit(solution)/shard_map/reduce_scatter | solution.py:96
  7.2 229.1 %collective-permute-start = (f32[5,32,32,256]{3,2,1,0:T(8,128)}, f32[5,32,32,256]{3,2,1,0:T(8,128)}, u32[]{:S(2)}, u32[]{:S(2)}) collective-permute-start(f32[5,32,32,256]{3,2,1,0:T(8,128)} %param.6), channel_id=1, source_target_pairs={{8,0},{16,8},{24,16},{32,24},{40,32},{48,40},{56,48},{64,56},{72,6... | collective-permute-start | bytes 15728648 | tf_op jit(solution)/shard_map/ppermute | solution.py:15
  8.5 227.8 %collective-permute-start.1 = (f32[5,32,32,256]{3,2,1,0:T(8,128)}, f32[5,32,32,256]{3,2,1,0:T(8,128)}, u32[]{:S(2)}, u32[]{:S(2)}) collective-permute-start(f32[5,32,32,256]{3,2,1,0:T(8,128)} %param.6), channel_id=1, source_target_pairs={{16,0},{24,8},{32,16},{40,24},{48,32},{56,40},{64,48},{72,56},{80,... | collective-permute-start | bytes 15728648 | tf_op jit(solution)/shard_map/ppermute | solution.py:15
  282.3 22.6 %slice-start = ((s8[5242880]{0:T(1024)(128)(4,1)}), s8[1048576]{0:T(1024)(128)(4,1)S(1)}, s32[]{:S(2)}) async-start(s8[5242880]{0:T(1024)(128)(4,1)} %bitcast.48), calls=%async_computation.4 | async-start | bytes 2097152
  291.2 13.8 %slice-start.1 = ((s8[5242880]{0:T(1024)(128)(4,1)}), s8[4194304]{0:T(1024)(128)(4,1)S(1)}, s32[]{:S(2)}) async-start(s8[5242880]{0:T(1024)(128)(4,1)} %bitcast.48), calls=%async_computation.5 | async-start | bytes 8388608
  291.2 26.4 %slice-start.6 = ((s8[5242880]{0:T(1024)(128)(4,1)}), s8[4194304]{0:T(1024)(128)(4,1)S(1)}, s32[]{:S(2)}) async-start(s8[5242880]{0:T(1024)(128)(4,1)} %bitcast.67), calls=%async_computation.10 | async-start | bytes 8388608
  304.9 12.6 %slice-start.7 = ((s8[5242880]{0:T(1024)(128)(4,1)}), s8[1048576]{0:T(1024)(128)(4,1)S(1)}, s32[]{:S(2)}) async-start(s8[5242880]{0:T(1024)(128)(4,1)} %bitcast.67), calls=%async_computation.11 | async-start | bytes 2097152
  304.9 22.5 %slice-start.4 = ((s8[5242880]{0:T(1024)(128)(4,1)}), s8[4194304]{0:T(1024)(128)(4,1)S(1)}, s32[]{:S(2)}) async-start(s8[5242880]{0:T(1024)(128)(4,1)} %bitcast.65), calls=%async_computation.8 | async-start | bytes 8388608
  317.5 9.9 slice-start.5
  317.5 19.5 %slice-start.2 = ((s8[5242880]{0:T(1024)(128)(4,1)}), s8[4194304]{0:T(1024)(128)(4,1)S(1)}, s32[]{:S(2)}) async-start(s8[5242880]{0:T(1024)(128)(4,1)} %bitcast.63), calls=%async_computation.6 | async-start | bytes 8388608
  327.4 9.7 slice-start.3
  347.0 143.6 %collective-permute-start.2 = (f32[5,5,256,256]{2,3,0,1:T(8,128)}, f32[5,5,256,256]{2,3,0,1:T(8,128)}, u32[]{:S(2)}, u32[]{:S(2)}) collective-permute-start(f32[5,5,256,256]{2,3,0,1:T(8,128)} %fusion.63), channel_id=1, source_target_pairs={{0,8},{8,16},{16,24},{24,32},{32,40},{40,48},{48,56},{56,64},{64,7... | collective-permute-start | bytes 19660808 | tf_op jit(solution)/shard_map/ppermute | solution.py:15
  354.1 277.0 %collective-permute-start.3 = (f32[5,5,256,256]{2,3,0,1:T(8,128)}, f32[5,5,256,256]{2,3,0,1:T(8,128)}, u32[]{:S(2)}, u32[]{:S(2)}) collective-permute-start(f32[5,5,256,256]{2,3,0,1:T(8,128)} %fusion.63), channel_id=1, source_target_pairs={{0,16},{8,24},{16,32},{24,40},{32,48},{40,56},{48,64},{56,72},{64,... | collective-permute-start | bytes 19660808 | tf_op jit(solution)/shard_map/ppermute | solution.py:15
  472.1 9.9 copy-start
  472.1 12.7 %copy-start.1 = (s32[64]{0:T(128)S(1)}, s32[64]{0:T(128)}, u32[]{:S(2)}) copy-start(s32[64]{0:T(128)} %param.8) | copy-start | bytes 772
  481.7 572.0 %reduce-scatter.3.cloned.1.call-start = ((), (), s32[]{:S(2)}) async-start(), calls=%async_computation.2 | async-start | bytes 14745600 | tf_op jit(solution)/shard_map/reduce_scatter | solution.py:95
Sparse Core Ops, SparseCore 0:
  481.8 29.1 reduce-scatter.4
  722.3 331.3 reduce-scatter.2
where the time goes:
time: 1070 us; the launch traced here: 1060 us
  waiting for transfers between devices  693 us (65%)
  starting transfers between devices  127 us (12%)
  local copies, waits for them, and re-layouts  94.5 us (9%)
  other arithmetic  65.6 us (6%)
  matrix products  65.3 us (6%)
  between operations  14.8 us (1%)
    ppermute x4, waiting for transfers between devices, from_behind_2(): lax.ppermute(value, axis, [(source, source + steps) for source in range(i...  362 us
    reduce_scatter x1, waiting for transfers between devices, local(): lax.psum_scatter(chosen, 'aux', scatter_dimension=2, tiled=True)  331 us
    ppermute x4, starting transfers between devices, from_behind_2(): lax.ppermute(value, axis, [(source, source + steps) for source in range(i...  127 us
    dot_general x6, matrix products, outer_sum(): jnp.einsum('spm,spn->smn', left, right, precision=lax.Precision.HIGHEST,...  65.3 us
    gather x5, local copies, waits for them, and re-layouts, local(): jnp.take(window, place, axis=0)  43.5 us
    concatenate x1, local copies, waits for them, and re-layouts, local(): jnp.concatenate([upper_pairs] + from_behind, axis=0)  21.5 us
  transfers between devices with their start and end apart: 6, of which 4 were waited for; matrix products, arithmetic and copies ran while one was open for 11% of the time, Pallas kernels for 0%

commit v1 on v0

v1 whole, which is shorter than its diff:
```python
import functools
import math

import jax
import jax.numpy as jnp
import numpy as np
from jax import lax
from jax.experimental import pallas as pl
from jax.experimental.pallas import tpu as pltpu
from jax.sharding import PartitionSpec as P

MESH = pl.DeviceIdType.MESH
F32, BF16, I32 = jnp.float32, jnp.bfloat16, jnp.int32

SLOTS = 5
REACH = 5
RANKS = 8
ZDIM = 4
SHARD = 32

A1, A2, B1, B2, A3, B3 = 5, 6, 7, 8, 9, 10
FRONT, BACK = 16, 32


def _plan():
    near = [(t, t + d) for d in (1, 2) for t in range(SLOTS - d)]
    far = [(t, t + d) for d in (3, 4) for t in range(SLOTS - d)] + [(t, t) for t in range(SLOTS)]
    first = [(A1, BACK + s) for s in range(4)] + [(B1, FRONT + t) for t in (1, 2, 3)]
    second = [(A1, BACK + 4), (A2, BACK + 2), (A2, BACK + 3), (B1, FRONT + 4)]
    second += [(B2, FRONT + t) for t in (1, 2, 3)]
    last = [(A3, BACK + 2), (B3, FRONT + 2)]
    return [near, far, first, second, last]


PLAN = _plan()
SIZES = [len(group) for group in PLAN]
OFFS = [sum(SIZES[:g]) for g in range(len(PLAN))]
TOTAL = sum(SIZES)
QUADS = [2, 1, 2, 2, 1]
QOFFS = [sum(QUADS[:g]) for g in range(len(PLAN))]
NQUAD = sum(QUADS)
AHEAD = [0, 0, 4, 3, 1]
BEHIND = [0, 0, 3, 4, 1]
RES_T = 36
RES_FA = RES_T + 4 * NQUAD
RES_FB = RES_FA + 12
ZERO = RES_FB + 12
NRES = ZERO + 1


def _tables():
    row, column, from_a, from_b = {}, {}, {}, {}
    for g, group in enumerate(PLAN):
        for i, key in enumerate(group):
            row[key] = OFFS[g] + i
            column[key] = RES_T + 4 * QOFFS[g] + i
            if g >= 2 and i < AHEAD[g]:
                from_a[key] = RES_FA + 4 * (g - 2) + i
            elif g >= 2:
                from_b[key] = RES_FB + 4 * (g - 2) + i - AHEAD[g]
    table = np.full((3, SLOTS, 2 * REACH + 1, 2), ZERO, np.int32)
    aheads, behinds = (A1, A2, A3), (B1, B2, B3)
    for n in (3, 4, 5):
        for t in range(n):
            for d in range(1, REACH + 1):
                p = t + d
                if p < n:
                    places = [row[(t, p)]]
                else:
                    k, s = p - n + 1, n - 1 - t
                    places = []
                    if k <= 3 and (aheads[k - 1], BACK + s) in column:
                        places.append(column[(aheads[k - 1], BACK + s)])
                    if s <= 2 and (behinds[s], FRONT + k - 1) in from_b:
                        places.append(from_b[(behinds[s], FRONT + k - 1)])
                assert len(places) == (2 if p >= n and (k, s) == (3, 2) else 1), (n, t, d)
                table[n - 3, t, REACH + d, : len(places)] = places
                q = t - d
                if q >= 0:
                    places = [column[(q, t)]]
                else:
                    k = -q
                    places = []
                    if k <= 3 and (behinds[k - 1], FRONT + t) in column:
                        places.append(column[(behinds[k - 1], FRONT + t)])
                    if t <= 2 and (aheads[t], BACK + k - 1) in from_a:
                        places.append(from_a[(aheads[t], BACK + k - 1)])
                assert len(places) == (2 if q < 0 and (k, t) == (3, 2) else 1), (n, t, -d)
                table[n - 3, t, REACH - d, : len(places)] = places
    return table.reshape(-1)


TABLE = _tables()
NTAB = TABLE.shape[0]
LEFT = np.array([key[0] for group in PLAN for key in group], np.int32)
RIGHT = np.array([key[1] for group in PLAN for key in group], np.int32)
CONSTS = np.concatenate([TABLE, LEFT, RIGHT])


def kernel(
    blk_count,
    owner_ref,
    partners_ref,
    consts_ref,
    fac_ref,
    pair_ref,
    diag_ref,
    own,
    staged,
    inbox,
    left_hi,
    left_lo,
    right_hi,
    right_lo,
    lhalf_hi,
    lhalf_lo,
    parts,
    from_core,
    out_across,
    out_up,
    out_down,
    relay_up,
    relay_down,
    sum_up,
    sum_down,
    rows_of,
    from_before,
    from_after,
    t_out,
    t_in,
    res,
    right_at,
    place_at,
    own_sem,
    y_send,
    y_recv,
    c_send,
    c_recv,
    z1_send,
    z1_recv,
    z2_send,
    z2_recv,
    t_send,
    t_recv,
    f_send,
    f_recv,
):
    depth = own.shape[1]
    half = depth // 2
    blocks = owner_ref.shape[0]
    partner_slots = partners_ref.shape[1]
    scale = 1.0 / math.sqrt(RANKS * depth)

    b, r = lax.axis_index("blk"), lax.axis_index("aux")
    z, c = r // 2, r % 2
    after, before = (b + 1) % blk_count, (b + blk_count - 1) % blk_count
    up, down, across = (z + 1) % ZDIM, (z + 3) % ZDIM, (z + 2) % ZDIM
    dev_after, dev_before = (after, r), (before, r)
    dev_core = (b, 2 * z + 1 - c)
    dev_up, dev_down = (b, 2 * up + c), (b, 2 * down + c)

    own_copies = [pltpu.make_async_copy(fac_ref.at[t], own.at[t], own_sem.at[t]) for t in range(SLOTS)]
    for t in (4, 3, 2, 1, 0):
        own_copies[t].start()

    barrier = pltpu.get_barrier_semaphore()
    peers = [(b, (r + k) % RANKS) for k in range(1, RANKS)] + [dev_after, dev_before]
    for peer in peers:
        pl.semaphore_signal(barrier, inc=1, device_id=peer, device_id_type=MESH)

    def tally(i, carry):
        count, first = carry
        holder = owner_ref[i]
        return count + (holder == b).astype(I32), first + (holder < b).astype(I32)

    count, first = lax.fori_loop(0, blocks, tally, (jnp.int32(0), jnp.int32(0)))
    count = jnp.clip(count, 3, SLOTS)

    pl.semaphore_wait(barrier, len(peers))

    def remote(src, dst, send, recv, device):
        return pltpu.make_async_remote_copy(
            src_ref=src, dst_ref=dst, send_sem=send, recv_sem=recv, device_id=device, device_id_type=MESH
        )

    sends_a = [
        remote(fac_ref.at[0], inbox[0], y_send.at[0], y_recv.at[0], dev_before),
        remote(fac_ref.at[1], inbox[1], y_send.at[1], y_recv.at[1], dev_before),
        remote(fac_ref.at[2, pl.ds(0, half)], inbox[2], y_send.at[2], y_recv.at[2], dev_before),
    ]
    sends_b = [
        remote(staged[k], inbox[3 + k], y_send.at[3 + k], y_recv.at[3 + k], dev_after) for k in range(3)
    ]
    sends_a[0].start()
    for t in (4, 3, 2, 1, 0):
        own_copies[t].wait()

    for k in range(3):
        start = half if k == 2 else 0

        def stage(i, _, k=k, start=start):
            rows = pl.ds(pl.multiple_of(i * 64, 64), 64)
            staged[k][rows, :] = own[count - 1 - k, pl.ds(pl.multiple_of(start + i * 64, 64), 64), :]
            return 0

        lax.fori_loop(0, (depth - start) // 64, stage, 0)
        sends_b[k].start()
        if k < 2:
            sends_a[k + 1].start()

    def right_of(e, _):
        code = consts_ref[NTAB + TOTAL + e]
        s, t = code - BACK, code - FRONT
        from_back = jnp.where(s < count, count - 1 - s, B1 + s - count)
        from_front = jnp.where(t < count, t, A1 + t - count)
        right = jnp.where(code >= BACK, from_back, jnp.where(code >= FRONT, from_front, code))
        right_at[e] = jnp.clip(right, 0, B2)
        return 0

    lax.fori_loop(0, TOTAL, right_of, 0)

    def place_of(i, _):
        t, j = i // partner_slots, i % partner_slots
        a = jnp.clip(first + t, 0, blocks - 1)
        partner = partners_ref[a, j]
        d = jnp.clip(partner - a, -REACH, REACH)
        ok = (partner >= 0) & (t < count)
        at = (((count - 3) * SLOTS + t) * (2 * REACH + 1) + d + REACH) * 2
        at = jnp.clip(at, 0, NTAB - 2)
        place_at[2 * i] = jnp.where(ok, consts_ref[at], ZERO)
        place_at[2 * i + 1] = jnp.where(ok, consts_ref[at + 1], ZERO)
        return 0

    lax.fori_loop(0, SLOTS * partner_slots, place_of, 0)
    res[ZERO] = jnp.zeros(res.shape[1:], F32)

    step = 128

    def split(x):
        hi = x.astype(BF16)
        return hi, (x - hi.astype(F32)).astype(BF16)

    def prepare(load, at):
        def body(i, _):
            rows = pl.ds(pl.multiple_of(i * step, step), step)
            x = load(rows)
            right_hi[at, rows, :], right_lo[at, rows, :] = split(x)
            left_hi[at, :, rows], left_lo[at, :, rows] = split(x.T)
            return 0

        lax.fori_loop(0, depth // step, body, 0)

    def prepare_half(k):
        def body(i, _):
            rows = pl.ds(pl.multiple_of(i * step, step), step)
            lhalf_hi[k, :, rows], lhalf_lo[k, :, rows] = split(inbox[2 + 3 * k][rows, :].T)
            return 0

        lax.fori_loop(0, half // step, body, 0)

    def times(lh, ll, rh, rl):
        total = jnp.dot(lh, rh, preferred_element_type=F32)
        total += jnp.dot(lh, rl, preferred_element_type=F32)
        return total + jnp.dot(ll, rh, preferred_element_type=F32)

    def store(total, g, i):
        for rank in range(RANKS):
            parts[g][rank % 2, rank // 2, i] = total[rank * SHARD : (rank + 1) * SHARD]

    def over(g, body):
        def run(i, _):
            body(i)
            return 0

        lax.fori_loop(0, SIZES[g], run, 0)

    def products(g):
        def body(i):
            left, right = jnp.clip(consts_ref[NTAB + OFFS[g] + i], 0, B2), right_at[OFFS[g] + i]
            store(times(left_hi[left], left_lo[left], right_hi[right], right_lo[right]), g, i)

        over(g, body)

    def products_half(g):
        for k in range(2):
            right, rows = right_at[OFFS[g] + k], pl.ds(k * half, half)
            store(times(lhalf_hi[k], lhalf_lo[k], right_hi[right, rows, :], right_lo[right, rows, :]), g, k)

    def core_copy(g):
        return remote(parts[g].at[1 - c], from_core[g], c_send.at[g], c_recv.at[g], dev_core)

    def relay_copies(g):
        upper, lower = out_across[g].at[:, pl.ds(0, 16)], out_across[g].at[:, pl.ds(16, 16)]
        return (
            remote(upper, relay_up[g], z1_send.at[g, 0], z1_recv.at[g, 0], dev_up),
            remote(lower, relay_down[g], z1_send.at[g, 1], z1_recv.at[g, 1], dev_down),
        )

    def sum_copies(g):
        return (
            remote(out_up[g], sum_up[g], z2_send.at[g, 0], z2_recv.at[g, 0], dev_up),
            remote(out_down[g], sum_down[g], z2_send.at[g, 1], z2_recv.at[g, 1], dev_down),
        )

    def add_core(g):
        core_copy(g).wait_recv()

        def add_across(i):
            out_across[g][i] = parts[g][c, across, i] + from_core[g][across, i]

        over(g, add_across)
        for copy in relay_copies(g):
            copy.start()

    def add_relay(g):
        for copy in relay_copies(g):
            copy.wait_recv()

        def add(i):
            total = parts[g][c, up, i] + from_core[g][up, i]
            out_up[g][i, :16, :] = total[:16] + relay_up[g][i]
            out_up[g][i, 16:, :] = total[16:]
            total = parts[g][c, down, i] + from_core[g][down, i]
            out_down[g][i, :16, :] = total[:16]
            out_down[g][i, 16:, :] = total[16:] + relay_down[g][i]

        over(g, add)
        for copy in sum_copies(g):
            copy.start()

    def forward_copies(g):
        if not AHEAD[g]:
            return ()
        ahead, behind = pl.ds(0, AHEAD[g]), pl.ds(AHEAD[g], BEHIND[g])
        return (
            remote(rows_of[g].at[ahead], from_before[g - 2], f_send.at[g, 0], f_recv.at[g, 0], dev_after),
            remote(rows_of[g].at[behind], from_after[g - 2], f_send.at[g, 1], f_recv.at[g, 1], dev_before),
        )

    def turn_copy(g, k):
        to = (r + k) % RANKS
        return remote(t_out[g].at[to], t_in[g].at[r], t_send.at[g, k], t_recv.at[g, k], (b, to))

    def turn_arrival(g, k):
        to, source = (r + k) % RANKS, (r + RANKS - k) % RANKS
        return remote(t_out[g].at[to], t_in[g].at[source], t_send.at[g, k], t_recv.at[g, k], (b, to))

    def finish(g):
        for copy in sum_copies(g):
            copy.wait_recv()

        def add(i):
            total = (parts[g][c, z, i] + from_core[g][z, i]) + (sum_up[g][i] + sum_down[g][i])
            res[OFFS[g] + i] = total
            rows_of[g][i] = total

        over(g, add)
        for copy in forward_copies(g):
            copy.start()

        for q in range(QUADS[g]):
            at = OFFS[g] + 4 * q
            turned = res[at : at + 4].reshape(4 * SHARD, RANKS * SHARD).T
            for rank in range(RANKS):
                t_out[g][rank, q] = turned[rank * SHARD : (rank + 1) * SHARD]

        def send(k, _):
            turn_copy(g, k).start()
            return 0

        lax.fori_loop(1, RANKS, send, 0)

    def collect(g):
        def arrive(k, _):
            turn_arrival(g, k).wait_recv()
            return 0

        lax.fori_loop(1, RANKS, arrive, 0)
        t_in[g][r] = t_out[g][r]
        for q in range(QUADS[g]):
            pieces = [t_in[g][rank, q] for rank in range(RANKS)]
            for i in range(4):
                lanes = slice(SHARD * i, SHARD * (i + 1))
                at = RES_T + 4 * (QOFFS[g] + q) + i
                res[at] = jnp.concatenate([piece[:, lanes] for piece in pieces], axis=1)

    def prepare_own(t, _):
        prepare(lambda rows: own[t, rows, :], t)
        return 0

    lax.fori_loop(0, SLOTS, prepare_own, 0)
    for g in (0, 1):
        products(g)
        core_copy(g).start()
    for g in (0, 1):
        add_core(g)
    for g in (0, 1):
        add_relay(g)
    for g in (0, 1):
        finish(g)

    def arrived(k):
        sends_a[k].wait_recv()
        sends_b[k].wait_recv()

    def prepare_in(k):
        prepare(lambda rows: inbox[k][rows, :], A1 + k)
        prepare(lambda rows: inbox[3 + k][rows, :], B1 + k)

    arrived(0)
    prepare_in(0)
    products(2)
    core_copy(2).start()
    for g in (0, 1):
        collect(g)
    add_core(2)
    add_relay(2)
    finish(2)

    arrived(1)
    prepare_in(1)
    products(3)
    core_copy(3).start()
    collect(2)
    add_core(3)

    arrived(2)
    for k in range(2):
        prepare_half(k)
    products_half(4)
    core_copy(4).start()
    add_relay(3)
    add_core(4)
    finish(3)
    add_relay(4)
    finish(4)
    collect(3)
    collect(4)
    for g in (2, 3, 4):
        for copy in forward_copies(g):
            copy.wait_recv()
        for i in range(AHEAD[g]):
            res[RES_FA + 4 * (g - 2) + i] = from_before[g - 2][i]
        for i in range(BEHIND[g]):
            res[RES_FB + 4 * (g - 2) + i] = from_after[g - 2][i]

    def place(i, _):
        block = res[place_at[2 * i]] + res[place_at[2 * i + 1]]
        pair_ref[i // partner_slots, i % partner_slots] = block * scale
        return 0

    lax.fori_loop(0, SLOTS * partner_slots, place, 0)

    def place_diag(t, _):
        at = jnp.where(t < count, OFFS[1] + 3 + t, ZERO)
        diag_ref[t] = res[at] * scale
        return 0

    lax.fori_loop(0, SLOTS, place_diag, 0)

    for copy in sends_a + sends_b:
        copy.wait_send()
    for g in range(len(PLAN)):
        for copy in (core_copy(g), *relay_copies(g), *sum_copies(g), *forward_copies(g)):
            copy.wait_send()

        def sent(k, _, g=g):
            turn_copy(g, k).wait_send()
            return 0

        lax.fori_loop(1, RANKS, sent, 0)


def local(blk_count, factors, partners, block_owner):
    slots, aux_dev, occ, nb = factors.shape
    depth = aux_dev * occ
    half = depth // 2
    groups = len(PLAN)
    dma = pltpu.SemaphoreType.DMA
    smem, vmem = pl.BlockSpec(memory_space=pltpu.SMEM), pl.BlockSpec(memory_space=pltpu.VMEM)

    def room(*shape):
        return pltpu.VMEM((*shape, nb), F32)

    def by_group(*lead, rows=SHARD, sizes=SIZES):
        return [room(*lead, size, rows) for size in sizes]

    return pl.pallas_call(
        functools.partial(kernel, blk_count),
        out_shape=[
            jax.ShapeDtypeStruct((slots, partners.shape[1], SHARD, nb), F32),
            jax.ShapeDtypeStruct((slots, SHARD, nb), F32),
        ],
        in_specs=[smem, smem, smem, pl.BlockSpec(memory_space=pl.ANY)],
        out_specs=[vmem, vmem],
        scratch_shapes=[
            room(slots, depth),
            [room(depth), room(depth), room(half)],
            [room(depth), room(depth), room(half)] * 2,
            pltpu.VMEM((9, nb, depth), BF16),
            pltpu.VMEM((9, nb, depth), BF16),
            pltpu.VMEM((9, depth, nb), BF16),
            pltpu.VMEM((9, depth, nb), BF16),
            pltpu.VMEM((2, nb, half), BF16),
            pltpu.VMEM((2, nb, half), BF16),
            by_group(2, ZDIM),
            by_group(ZDIM),
            by_group(),
            by_group(),
            by_group(),
            by_group(rows=SHARD // 2),
            by_group(rows=SHARD // 2),
            by_group(),
            by_group(),
            by_group(),
            by_group(sizes=AHEAD[2:]),
            by_group(sizes=BEHIND[2:]),
            [pltpu.VMEM((RANKS, quads, SHARD, 4 * SHARD), F32) for quads in QUADS],
            [pltpu.VMEM((RANKS, quads, SHARD, 4 * SHARD), F32) for quads in QUADS],
            room(NRES, SHARD),
            pltpu.SMEM((TOTAL,), I32),
            pltpu.SMEM((2 * slots * partners.shape[1],), I32),
            dma((SLOTS,)),
            dma((6,)),
            dma((6,)),
            dma((groups,)),
            dma((groups,)),
            dma((groups, 2)),
            dma((groups, 2)),
            dma((groups, 2)),
            dma((groups, 2)),
            dma((groups, RANKS)),
            dma((groups, RANKS)),
            dma((groups, 2)),
            dma((groups, 2)),
        ],
        compiler_params=pltpu.CompilerParams(
            collective_id=0, has_side_effects=True, vmem_limit_bytes=60 * 1024 * 1024
        ),
    )(block_owner, partners, jnp.asarray(CONSTS), factors.reshape(slots, depth, nb))


def solution(mesh):
    in_specs = (P("blk", "aux", None, None), P(), P())
    out_specs = (P("blk", None, "aux", None), P("blk", "aux", None))
    return jax.shard_map(
        functools.partial(local, mesh.shape["blk"]),
        mesh=mesh,
        in_specs=in_specs,
        out_specs=out_specs,
        check_vma=False,
    )
```

time: 1070 us -> 104 us (0.10)
  waiting for transfers between devices: 693 us -> 0 us
  starting transfers between devices: 127 us -> 0 us
  Pallas kernels: 0 us -> 98.6 us
  local copies, waits for them, and re-layouts: 94.5 us -> 4.89 us
  other arithmetic: 65.6 us -> 0 us
  matrix products: 65.3 us -> 0 us
  between operations: 14.8 us -> 0.65 us
    ppermute x4 -> x0, waiting for transfers between devices: 362 us -> none  [from_behind_2(): lax.ppermute(value, axis, [(source, source + steps) for source in range(i...]
    reduce_scatter x2 -> x0, waiting for transfers between devices: 331 us -> none  [the longest x1 331 us: local(): lax.psum_scatter(chosen, 'aux', scatter_dimension=2, tiled=True)]
    ppermute x4 -> x0, starting transfers between devices: 127 us -> none  [from_behind_2(): lax.ppermute(value, axis, [(source, source + steps) for source in range(i...]
    pallas_call x0 -> x1, Pallas kernels: none -> 98.6 us  [local(): pl.pallas_call(functools.partial(kernel, blk_count), out_shape=[jax.Shape...]
    dot_general x6 -> x0, matrix products: 65.3 us -> none  [outer_sum(): jnp.einsum('spm,spn->smn', left, right, precision=lax.Precision.HIGHEST,...]
    gather x7 -> x0, local copies, waits for them, and re-layouts: 58.4 us -> none  [the longest x5 43.5 us: local(): jnp.take(window, place, axis=0)]
    concatenate x2 -> x0, other arithmetic: 26.7 us -> none  [the longest x1 15.3 us: local(): jnp.concatenate([upper_pairs] + from_behind, axis=0)]
    concatenate x1 -> x0, local copies, waits for them, and re-layouts: 21.5 us -> none  [local(): jnp.concatenate([upper_pairs] + from_behind, axis=0)]
  transfers between devices with their start and end apart: 6 -> 0, of which waited for: 4 -> 0; matrix products, arithmetic and copies ran while one was open for 11% -> 0% of each run, Pallas kernels for 0% -> 0%
where the time goes in v1:
time: 104 us
  Pallas kernels  98.6 us (95%)
  local copies, waits for them, and re-layouts  4.89 us (5%)
    pallas_call x1, Pallas kernels, local(): pl.pallas_call(functools.partial(kernel, blk_count), out_shape=[jax.Shape...  98.6 us
    unnamed x5, local copies, waits for them, and re-layouts  4.89 us

profile of v1, /device:TPU:1, one launch (start us, length us, event | category | flops | bytes accessed | tf_op | source)
XLA Modules:
  0.0 104.1 jit_solution(8027773320164312398)
XLA Ops:
  0.6 1.4 %copy.6.partners_ref = s32[64,10]{1,0:T(8,128)} copy(s32[64,10]{0,1:T(8,128)} %param.5) | data formatting | bytes 5120 | tf_op args[1]
  2.0 98.6 %shard_map.59 = (f32[5,10,32,256]{3,2,1,0:T(8,128)}, f32[5,32,256]{2,1,0:T(8,128)}) custom-call(s32[64]{0:T(128)} %owner_ref.1, s32[64,10]{1,0:T(8,128)} %copy.6.partners_ref, s32[392]{0:T(512)} %constant.2.clone.consts_ref, f32[5,1024,256]{2,1,0:T(8,128)} %bitcast.1), custom_call_target="tpu_custom_call" | custom-call | tf_op jit(solution)/shard_map/pallas_call | solution.py:488
  100.6 0.0 copy-start
  100.6 2.8 %copy.9 = f32[5,10,32,256]{3,2,1,0:T(8,128)} copy(f32[5,10,32,256]{3,2,1,0:T(8,128)} %get-tuple-element.4) | data formatting | bytes 3276800
  103.5 0.0 copy-done
  103.5 0.7 copy.10
Async XLA Ops:
  100.6 2.8 %copy-start = (f32[5,32,256]{2,1,0:T(8,128)S(1)}, f32[5,32,256]{2,1,0:T(8,128)}, u32[]{:S(2)}) copy-start(f32[5,32,256]{2,1,0:T(8,128)} %get-tuple-element.5) | copy-start | bytes 491524
